TPU v7x, 32 devices: a whole 2x2x4 slice. The times are simulated.
32 devices in a mesh: case: 2 (over x), mesh: 8 (over z, y), harm: 2 (over core).
Axes of the slice: x: 2, y: 2, z: 4, core: 2. Of those that a mesh axis runs over, the one named last changes fastest.
Arguments:
- coeffs: float32 [64, 3, 16384], P('harm', None, ('case', 'mesh')), parts along dimension 2, may hold values from -0.2 to 0.2
- load: float32 [64, 3, 16384], P('harm', None, ('case', 'mesh')), parts along dimension 2, may hold values from -2 to 2
- mass: float32 [8192], P('mesh'), may hold values from 0.3 to 3
- stiffness: float32 [16384], P('mesh'), may hold values from 0.3 to 3
- edge_ref: float32 [2, 3, 16384], P(None, None, 'mesh'), may hold values from -4 to 4
- conn: int32 [3, 16384], P(None, 'mesh'), may hold values from 0 to 1151, as said below
- ghost_send: int32 [2, 512], P(None, 'mesh'), may hold values from 0 to 1023
- order: int32 [64], replicated, may hold values from 0 to 63, each once
- basis: bfloat16 [256, 3, 8192], P(None, None, 'mesh'), may hold values from -0.0546875 to 0.0546875
Outputs:
- resid: float32 [64, 3, 16384], P('harm', None, ('case', 'mesh')), parts along dimension 2
- reduced: float32 [256, 128], P('mesh', ('case', 'harm')), parts along dimension 1
There are 2 independent parts, one for each index of `case`. A program takes and returns all parts, laid end to end along the dimension named above; an argument that names none is the same for every part. Nothing has to cross between parts.
Inputs may be any that keep to these rules, and one draw needn't show every extreme that they name: `conn`: A triangle of the first block refers to no lower neighbour node slot, one of the last block to no upper one; slots 1024 to 1087 name the lower neighbour's shared nodes, the rest the upper neighbour's.
All inputs are finite; a program needn't handle non-finite values.
Results may differ from a plain program's by a relative error of at most 0.003.
Values sent between devices are 32-bit elements; how exact they have to be, the bound alone decides.
A program may use at most 64 MiB of HBM per device.

v0:
```python
import math

import jax
import jax.numpy as jnp
from jax import lax
from jax.sharding import PartitionSpec as P

OMEGA = 0.1
PRESTRESS = 0.2


def extended_2(shard, sides, width):
    for axis, dim in sides:
        devices, length = (lax.axis_size(axis), shard.shape[dim])
        up = [(i, (i + 1) % devices) for i in range(devices - 1)]
        down = [(j, i) for i, j in up]
        last = lax.slice_in_dim(shard, length - width, length, axis=dim)
        first = lax.slice_in_dim(shard, 0, width, axis=dim)
        before = lax.ppermute(last, axis, up)
        after = lax.ppermute(first, axis, down)
        shard = jnp.concatenate([before, shard, after], axis=dim)
    return shard


def fourier_tables(order, ncoef):
    samples = jnp.arange(ncoef, dtype=jnp.int32)
    harmonic = (order + 1) // 2
    phase = harmonic[:, None] * samples[None, :] % ncoef
    angle = 2.0 * math.pi / ncoef * phase.astype(jnp.float32)
    cosine = (order % 2 == 1) | (order == 0)
    synth = jnp.where(cosine[:, None], jnp.cos(angle), jnp.sin(angle))
    weight = jnp.where((order == 0) | (order == ncoef - 1), 1.0, 2.0) / ncoef
    proj = synth * weight[:, None]
    freq = (OMEGA * harmonic.astype(jnp.float32)) ** 2
    return (synth, proj, freq)


def edge_force(stiffness, ref_edge, start_disp, end_disp):
    stretch = ref_edge[None] + end_disp - start_disp
    tension = stiffness[None, :] * (
        0.5 * (jnp.sum(stretch * stretch, 1) - jnp.sum(ref_edge * ref_edge, 0)[None, :]) + PRESTRESS
    )
    return tension[:, None, :] * stretch


def pick_rows(flat, table):
    return jnp.dot(flat, table, precision=lax.Precision.HIGHEST)


def spread_rows(flat, table):
    return lax.dot_general(flat, table, (((1,), (1,)), ((), ())), precision=lax.Precision.HIGHEST)


def internal_forces(disp, stiffness, edge_ref, conn, ghost_send):
    time_rows = disp.shape[0]
    node_count = disp.shape[2]
    ghost_count = ghost_send.shape[1]
    flat_disp = disp.reshape(time_rows * 3, node_count)
    node_ids = jnp.arange(node_count, dtype=jnp.int32)
    shared = jnp.concatenate([ghost_send[0], ghost_send[1]], 0)
    share_table = (node_ids[:, None] == shared[None, :]).astype(jnp.float32)
    packed = pick_rows(flat_disp, share_table).reshape(time_rows, 3, 2 * ghost_count)
    border = extended_2(packed, (("mesh", 2),), ghost_count)
    extended = jnp.concatenate(
        [disp, border[:, :, :ghost_count], border[:, :, 3 * ghost_count :]], 2
    )
    slot_count = extended.shape[2]
    flat_ext = extended.reshape(time_rows * 3, slot_count)
    slot_ids = jnp.arange(slot_count, dtype=jnp.int32)
    table_first = (slot_ids[:, None] == conn[0][None, :]).astype(jnp.float32)
    table_second = (slot_ids[:, None] == conn[1][None, :]).astype(jnp.float32)
    table_third = (slot_ids[:, None] == conn[2][None, :]).astype(jnp.float32)
    elem_count = conn.shape[1]
    disp_first = pick_rows(flat_ext, table_first).reshape(time_rows, 3, elem_count)
    disp_second = pick_rows(flat_ext, table_second).reshape(time_rows, 3, elem_count)
    disp_third = pick_rows(flat_ext, table_third).reshape(time_rows, 3, elem_count)
    edge_one = edge_ref[0]
    edge_two = edge_ref[1]
    force_ab = edge_force(stiffness, edge_one, disp_first, disp_second)
    force_ac = edge_force(stiffness, edge_two, disp_first, disp_third)
    force_bc = edge_force(stiffness, edge_two - edge_one, disp_second, disp_third)
    on_first = (-force_ab - force_ac).reshape(time_rows * 3, elem_count)
    on_second = (force_ab - force_bc).reshape(time_rows * 3, elem_count)
    on_third = (force_ac + force_bc).reshape(time_rows * 3, elem_count)
    summed = (
        spread_rows(on_first, table_first)
        + spread_rows(on_second, table_second)
        + spread_rows(on_third, table_third)
    )
    summed = summed.reshape(time_rows, 3, slot_count)
    returned = extended_2(summed[:, :, node_count:], (("mesh", 2),), ghost_count)
    back = jnp.concatenate([returned[:, :, :ghost_count], returned[:, :, 3 * ghost_count :]], 2)
    added = spread_rows(back.reshape(time_rows * 3, 2 * ghost_count), share_table)
    owned = summed[:, :, :node_count] + added.reshape(time_rows, 3, node_count)
    return owned


def per_device(coeffs, load, mass, stiffness, edge_ref, conn, ghost_send, order, basis):
    harm_count = lax.axis_size("harm")
    harm_index = lax.axis_index("harm")
    coef_block = coeffs.shape[0]
    node_count = coeffs.shape[2]
    coef_total = coef_block * harm_count
    time_block = coef_total // harm_count
    synth, proj, freq = fourier_tables(order, coef_total)
    synth_mine = lax.dynamic_slice_in_dim(synth, harm_index * time_block, time_block, 1)
    block_in = lax.all_gather(coeffs, "harm", axis=0, tiled=True)
    flat_disp = jnp.dot(
        synth_mine.T, block_in.reshape(block_in.shape[0], -1), precision=lax.Precision.HIGHEST
    )
    disp = flat_disp.reshape(time_block, 3, node_count)
    forces = internal_forces(disp, stiffness, edge_ref, conn, ghost_send)
    proj_mine = lax.dynamic_slice_in_dim(proj, harm_index * time_block, time_block, 1)
    flat_forces = forces.reshape(time_block, -1)
    force_coef = lax.psum_scatter(
        jnp.dot(proj_mine, flat_forces, precision=lax.Precision.HIGHEST),
        "harm",
        scatter_dimension=0,
        tiled=True,
    ).reshape(coef_block, 3, node_count)
    freq_mine = lax.dynamic_slice_in_dim(freq, harm_index * coef_block, coef_block, 0)
    resid = force_coef - freq_mine[:, None, None] * mass[None, None, :] * coeffs - load
    resid_low = resid.astype(jnp.bfloat16)
    basis_count = basis.shape[0]
    partial_proj = lax.dot_general(
        basis.reshape(basis_count, -1),
        resid_low.reshape(coef_block, -1),
        (((1,), (1,)), ((), ())),
        preferred_element_type=jnp.float32,
    )
    summed_proj = lax.psum(partial_proj, "mesh")
    share_rows = basis_count // lax.axis_size("mesh")
    reduced = lax.dynamic_slice_in_dim(
        summed_proj, lax.axis_index("mesh") * share_rows, share_rows, 0
    )
    return (resid, reduced)


def solution(mesh):
    in_specs = (
        P("harm", None, ("case", "mesh")),
        P("harm", None, ("case", "mesh")),
        P("mesh"),
        P("mesh"),
        P(None, None, "mesh"),
        P(None, "mesh"),
        P(None, "mesh"),
        P(),
        P(None, None, "mesh"),
    )
    out_specs = (P("harm", None, ("case", "mesh")), P("mesh", ("case", "harm")))
    return jax.shard_map(
        per_device, mesh=mesh, in_specs=in_specs, out_specs=out_specs, check_vma=False
    )
```

profile of v0, /device:TPU:0, one launch (start us, length us, event | category | flops | bytes accessed | tf_op | source)
XLA Modules:
  0.0 131.0 jit_solution(17384764372548799608)
XLA Ops:
  7.2 0.8 multiply_multiply_fusion
  8.0 0.7 compare_or_fusion
  8.7 2.6 %all_gather.3 = f32[64,3,1024]{2,0,1:T(8,128)S(1)} all-gather(f32[32,3,1024]{2,0,1:T(8,128)} %param.9), channel_id=1, replica_groups=mesh['case'=2,'mesh'=8,'harm'=2] {'harm'}, dimensions={0}, use_global_device_ids=true | all-gather | bytes 1179648 | tf_op jit(solution)/shard_map/all_gather | solution.py:107
  11.3 0.8 slice_bitcast_fusion.1
  12.1 0.1 sine_select_fusion
  12.2 0.1 pad_add_fusion
  12.3 0.5 fusion.21
  12.8 0.4 fusion.27
  13.2 0.1 fusion.55
  13.3 4.8 %collective-permute-start = (f32[32,3,64]{2,0,1:T(8,128)S(1)}, f32[32,3,64]{2,0,1:T(8,128)S(1)}, u32[]{:S(2)}, u32[]{:S(2)}) collective-permute-start(f32[32,3,64]{2,0,1:T(8,128)S(1)} %get-tuple-element.32), channel_id=1, source_target_pairs={{0,2},{2,4},{4,6},{6,8},{8,10},{10,12},{12,14},{1,3},{3,5},{5,7},{... | collective-permute-start | bytes 73736 | tf_op jit(solution)/shard_map/ppermute | solution.py:19
  18.1 1.3 collective-permute-start.1
  19.5 0.1 multiply_reduce_fusion.5
  19.6 0.2 collective-permute-done
  19.8 4.3 %collective-permute-done.1 = f32[32,3,64]{2,0,1:T(8,128)S(1)} collective-permute-done((f32[32,3,64]{2,0,1:T(8,128)S(1)}, f32[32,3,64]{2,0,1:T(8,128)S(1)}, u32[]{:S(2)}, u32[]{:S(2)}) %collective-permute-start.1) | collective-permute-done | bytes 24608 | tf_op jit(solution)/shard_map/ppermute | solution.py:20
  24.1 0.1 concatenate.14
  24.2 3.6 %fusion.10 = f32[32,3,2048]{2,0,1:T(8,128)S(1)} fusion(f32[32,3,1152]{2,0,1:T(8,128)S(1)} %concatenate.14, s32[2048]{0:T(1024)S(1)} %bitcast.75), kind=kOutput, calls=%fused_computation.11 | convolution fusion | flops 2720268288 | bytes 1236992 | tf_op jit(solution)/shard_map/dot_general | solution.py:47
  27.7 3.6 %fusion.6 = f32[32,3,2048]{2,0,1:T(8,128)S(1)} fusion(f32[32,3,1152]{2,0,1:T(8,128)S(1)} %concatenate.14, s32[2048]{0:T(1024)S(1)} %bitcast.73), kind=kOutput, calls=%fused_computation.9 | convolution fusion | flops 2720268288 | bytes 1236992 | tf_op jit(solution)/shard_map/dot_general | solution.py:47
  31.3 3.7 %multiply_reduce_fusion.2 = (f32[32,2048]{1,0:T(8,128)S(1)}, f32[32,3,2048]{2,0,1:T(8,128)S(1)}, f32[32,2048]{1,0:T(8,128)S(1)}, f32[32,3,2048]{2,0,1:T(8,128)S(...) fusion(f32[32,3,2048]{2,0,1:T(8,128)S(1)} %fusion.6, f32[3,2048]{1,0:T(4,128)S(1)} %bitcast.72, ...), kind=kOutput, calls=%fused_computation.31 | convolution fusion | flops 2722430976 | bytes 5242880 | tf_op jit(solution)/shard_map/dot_general | solution.py:47
  35.0 0.1 add_multiply_fusion.2
  35.1 1.1 multiply_subtract_fusion
  36.3 0.5 copy.18
  36.8 1.3 reshape.178
  38.1 7.0 %fusion.2 = f32[96,1152]{1,0:T(8,128)} fusion(f32[96,2048]{1,0:T(8,128)} %reshape.178, s32[2048]{0:T(1024)S(1)} %bitcast.78), kind=kOutput, calls=%fused_computation.4 | convolution fusion | flops 2720268288 | bytes 1236992 | tf_op jit(solution)/shard_map/dot_general | solution.py:51
  45.1 0.5 copy.20
  45.7 1.3 reshape.180
  47.0 6.8 %fusion = f32[96,1152]{1,0:T(8,128)} fusion(f32[96,2048]{1,0:T(8,128)} %reshape.180, s32[2048]{0:T(1024)S(1)} %bitcast.76), kind=kOutput, calls=%fused_computation.1 | convolution fusion | flops 2720268288 | bytes 1236992 | tf_op jit(solution)/shard_map/dot_general | solution.py:51
  53.7 0.5 copy.19
  54.3 0.4 reshape.179
  54.7 6.2 %fusion.19 = f32[96,1152]{1,0:T(8,128)S(1)} fusion(f32[96,1152]{1,0:T(8,128)} %fusion, f32[96,1152]{1,0:T(8,128)} %fusion.2, f32[96,2048]{1,0:T(8,128)S(1)} %reshape.179, s32[2048]{0:T(1024)S(1)} %bitcast.74), kind=kOutput, calls=%fused_computation.19 | convolution fusion | flops 2720489472 | bytes 2121728 | tf_op jit(solution)/shard_map/dot_general | solution.py:51
  60.9 0.2 reshape.181
  61.1 0.1 fusion.53
  61.2 4.3 %collective-permute-start.2 = (f32[32,3,64]{2,0,1:T(8,128)S(1)}, f32[32,3,64]{2,0,1:T(8,128)S(1)}, u32[]{:S(2)}, u32[]{:S(2)}) collective-permute-start(f32[32,3,64]{2,0,1:T(8,128)S(1)} %copy.34), channel_id=1, source_target_pairs={{0,2},{2,4},{4,6},{6,8},{8,10},{10,12},{12,14},{1,3},{3,5},{5,7},{... | collective-permute-start | bytes 73736 | tf_op jit(solution)/shard_map/ppermute | solution.py:19
  65.6 1.3 collective-permute-start.3
  66.9 0.1 slice.53
  67.0 0.3 collective-permute-done.2
  67.3 4.3 %collective-permute-done.3 = f32[32,3,64]{2,0,1:T(8,128)S(1)} collective-permute-done((f32[32,3,64]{2,0,1:T(8,128)S(1)}, f32[32,3,64]{2,0,1:T(8,128)S(1)}, u32[]{:S(2)}, u32[]{:S(2)}) %collective-permute-start.3) | collective-permute-done | bytes 24608 | tf_op jit(solution)/shard_map/ppermute | solution.py:20
  71.5 0.6 fusion.20
  72.2 1.7 %fusion.42 = f32[64,3072]{1,0:T(8,128)} fusion(f32[32,3072]{1,0:T(8,128)S(1)} %bitcast.71, f32[64,64]{0,1:T(8,128)S(1)} %sine_select_fusion, s32[]{:T(128)S(6)} %select_n.39, f32[64]{0:T(128)S(1)} %get-tuple-element.41), kind=kOutput, calls=%fused_computation.68 | convolution fusion | flops 75499520 | bytes 1196548 | tf_op jit(solution)/shard_map/dot_general | solution.py:116
  74.0 0.1 dynamic_slice.14
  74.0 0.1 broadcast_multiply_fusion
  74.1 8.5 %reduce-scatter.2.cloned.1.call-done = f32[32,3072]{1,0:T(8,128)} async-done(((f32[64,3072]{1,0:T(8,128)}), f32[32,3072]{1,0:T(8,128)}) %reduce-scatter.2.cloned.1.call-update) | async-done | bytes 393232 | tf_op jit(solution)/shard_map/reduce_scatter | solution.py:115
  82.6 1.3 reshape.183
  83.9 0.6 fusion.52
  84.5 1.0 copy.28
  85.5 0.6 convolution_bitcast_fusion
  86.1 37.3 %psum.7 = f32[256,32]{0,1:T(8,128)S(1)} all-reduce(f32[256,32]{0,1:T(8,128)S(1)} %convolution_bitcast_fusion), channel_id=1, replica_groups=mesh['case'=2,'mesh'=8,'harm'=2] {'mesh'}, use_global_device_ids=true, to_apply=%region_7.8 | all-reduce | flops 8192 | bytes 65536 | tf_op jit(solution)/shard_map/psum | solution.py:131
  123.4 0.1 constant_dynamic-slice_fusion
  123.5 0.7 copy.29
  (25 shorter events, 0.2 us)
Async XLA Ops:
  7.2 78.3 %copy-start = (bf16[256,3,1024]{2,0,1:T(8,128)(2,1)S(1)}, bf16[256,3,1024]{2,0,1:T(8,128)(2,1)}, u32[]{:S(2)}) copy-start(bf16[256,3,1024]{2,0,1:T(8,128)(2,1)} %param.17) | copy-start | bytes 4718596
  7.2 12.2 %copy-start.5 = (s32[3,2048]{1,0:T(4,128)S(1)}, s32[3,2048]{1,0:T(4,128)}, u32[]{:S(2)}) copy-start(s32[3,2048]{1,0:T(4,128)} %param.14) | copy-start | bytes 73732
  7.2 12.2 %copy-start.4 = (f32[2,3,2048]{2,0,1:T(2,128)S(1)}, f32[2,3,2048]{2,0,1:T(2,128)}, u32[]{:S(2)}) copy-start(f32[2,3,2048]{2,0,1:T(2,128)} %param.13) | copy-start | bytes 147460
  7.2 75.4 %reduce-scatter.2.cloned.1.call-start = ((), (), s32[]{:S(2)}) async-start(), calls=%async_computation.1 | async-start | bytes 1179648 | tf_op jit(solution)/shard_map/reduce_scatter | solution.py:115
  13.3 6.5 %collective-permute-start = (f32[32,3,64]{2,0,1:T(8,128)S(1)}, f32[32,3,64]{2,0,1:T(8,128)S(1)}, u32[]{:S(2)}, u32[]{:S(2)}) collective-permute-start(f32[32,3,64]{2,0,1:T(8,128)S(1)} %get-tuple-element.32), channel_id=1, source_target_pairs={{0,2},{2,4},{4,6},{6,8},{8,10},{10,12},{12,14},{1,3},{3,5},{5,7},{... | collective-permute-start | bytes 73736 | tf_op jit(solution)/shard_map/ppermute | solution.py:19
  18.1 6.0 %collective-permute-start.1 = (f32[32,3,64]{2,0,1:T(8,128)S(1)}, f32[32,3,64]{2,0,1:T(8,128)S(1)}, u32[]{:S(2)}, u32[]{:S(2)}) collective-permute-start(f32[32,3,64]{2,0,1:T(8,128)S(1)} %get-tuple-element.31), channel_id=1, source_target_pairs={{2,0},{4,2},{6,4},{8,6},{10,8},{12,10},{14,12},{3,1},{5,3},{7,5},{... | collective-permute-start | bytes 73736 | tf_op jit(solution)/shard_map/ppermute | solution.py:20
  31.3 3.7 %copy-start.6 = (f32[2048]{0:T(1024)S(1)}, f32[2048]{0:T(1024)}, u32[]{:S(2)}) copy-start(f32[2048]{0:T(1024)} %param.12) | copy-start | bytes 24580
  38.1 7.0 %copy-start.1 = (f32[32,3,2048]{2,0,1:T(8,128)S(1)}, f32[32,3,2048]{2,0,1:T(8,128)}, u32[]{:S(2)}) copy-start(f32[32,3,2048]{2,0,1:T(8,128)} %get-tuple-element.21) | copy-start | bytes 2359300
  61.2 6.1 %collective-permute-start.2 = (f32[32,3,64]{2,0,1:T(8,128)S(1)}, f32[32,3,64]{2,0,1:T(8,128)S(1)}, u32[]{:S(2)}, u32[]{:S(2)}) collective-permute-start(f32[32,3,64]{2,0,1:T(8,128)S(1)} %copy.34), channel_id=1, source_target_pairs={{0,2},{2,4},{4,6},{6,8},{8,10},{10,12},{12,14},{1,3},{3,5},{5,7},{... | collective-permute-start | bytes 73736 | tf_op jit(solution)/shard_map/ppermute | solution.py:19
  65.6 6.0 %collective-permute-start.3 = (f32[32,3,64]{2,0,1:T(8,128)S(1)}, f32[32,3,64]{2,0,1:T(8,128)S(1)}, u32[]{:S(2)}, u32[]{:S(2)}) collective-permute-start(f32[32,3,64]{2,0,1:T(8,128)S(1)} %copy.35), channel_id=1, source_target_pairs={{2,0},{4,2},{6,4},{8,6},{10,8},{12,10},{14,12},{3,1},{5,3},{7,5},{... | collective-permute-start | bytes 73736 | tf_op jit(solution)/shard_map/ppermute | solution.py:20
  72.1 1.9 %copy-start.7 = (f32[1024]{0:T(1024)S(1)}, f32[1024]{0:T(1024)}, u32[]{:S(2)}) copy-start(f32[1024]{0:T(1024)} %param.11) | copy-start | bytes 12292
  72.2 11.7 %copy-start.2 = (f32[32,3,1024]{2,0,1:T(8,128)S(1)}, f32[32,3,1024]{2,0,1:T(8,128)}, u32[]{:S(2)}) copy-start(f32[32,3,1024]{2,0,1:T(8,128)} %param.9) | copy-start | bytes 1179652
  72.2 11.7 %copy-start.3 = (f32[32,3,1024]{2,0,1:T(8,128)S(1)}, f32[32,3,1024]{2,0,1:T(8,128)}, u32[]{:S(2)}) copy-start(f32[32,3,1024]{2,0,1:T(8,128)} %param.10) | copy-start | bytes 1179652
Sparse Core Ops, SparseCore 0:
  74.1 8.4 reduce-scatter.1
where the time goes:
time: 131 us
  blocking collectives  40 us (31%)
  matrix products  34.6 us (26%)
  waiting for transfers between devices  17.5 us (13%)
  between operations  14.3 us (11%)
  starting transfers between devices  11.7 us (9%)
  local copies, waits for them, and re-layouts  9.16 us (7%)
  other arithmetic  3.74 us (3%)
    psum x1, blocking collectives, per_device(): summed_proj = lax.psum(partial_proj, 'mesh')  37.3 us
    dot_general x4, matrix products, spread_rows(): lax.dot_general(flat, table, (((1,), (1,)), ((), ())), precision=lax.Prec...  20.6 us
    dot_general x4, matrix products, pick_rows(): return jnp.dot(flat, table, precision=lax.Precision.HIGHEST)  11.2 us
    ppermute x2, starting transfers between devices, extended_2(): before = lax.ppermute(last, axis, up)  9.11 us
    ppermute x2, waiting for transfers between devices, extended_2(): after = lax.ppermute(first, axis, down)  8.52 us
    reduce_scatter x1, waiting for transfers between devices, per_device(): lax.psum_scatter(jnp.dot(proj_mine, flat_forces, precision=lax.Precision....  8.48 us
    all_gather x1, blocking collectives, per_device(): block_in = lax.all_gather(coeffs, 'harm', axis=0, tiled=True)  2.65 us
  transfers between devices with their start and end apart: 5, of which 5 were waited for; matrix products, arithmetic and copies ran while one was open for 0% of the time, Pallas kernels for 0%

commit v1 on v0

v1 whole, which is shorter than its diff:
```python
import math

import jax
import jax.numpy as jnp
from jax import lax
from jax.experimental import pallas as pl
from jax.experimental.pallas import tpu as pltpu
from jax.sharding import PartitionSpec as P

OMEGA = 0.1
PRESTRESS = 0.2
F32 = jnp.float32
BF16 = jnp.bfloat16
MESH = pl.DeviceIdType.MESH
LANES = 256


def halves(x):
    high = x.astype(BF16)
    return high, (x - high.astype(F32)).astype(BF16)


def dot(a, b):
    return jnp.dot(a, b, preferred_element_type=F32)


def dot_t(a, b):
    return lax.dot_general(a, b, (((1,), (1,)), ((), ())), preferred_element_type=F32)


def wave(order, samples, ncoef):
    harmonic = (order + 1) // 2
    phase = (harmonic * samples) % ncoef
    angle = (2.0 * math.pi / ncoef) * phase.astype(F32)
    cosine = (order % 2 == 1) | (order == 0)
    return jnp.where(cosine, jnp.cos(angle), jnp.sin(angle))


def kernel(
    n_mesh,
    coef_ref, load_hbm, mass_ref, stiff_ref, edge_ref, conn_ref, ghost_ref, order_ref, basis_hbm,
    resid_ref, reduced_ref,
    load_ref, basis_ref, coef_in, own_hl, other_hl, pick, inc, ghost_out, ghost_in, ghost_hl,
    edge_own, edge_hl, disp, force_hl, coef_hl, back_out, back_in, part_out, part_in, main_own, low,
    prod_out, prod_in,
    local_sem, coef_sem, ghost_send_sem, ghost_recv_sem, part_sem,
    back_send_sem, back_recv_sem, prod_send_sem, prod_recv_sem,
):
    rows, nodes = coef_ref.shape
    block = rows // 3
    ncoef = 2 * block
    ghosts = ghost_ref.shape[1]
    elems = conn_ref.shape[1] // 2
    slots = nodes + 2 * ghosts
    share = prod_out.shape[1]
    me = lax.axis_index("mesh")
    harm = lax.axis_index("harm")
    other = 1 - harm
    has_low, has_up = me > 0, me < n_mesh - 1

    barrier = pltpu.get_barrier_semaphore()
    pl.semaphore_signal(barrier, inc=1, device_id={"harm": other}, device_id_type=MESH)
    for step in range(1, n_mesh):
        pl.semaphore_signal(
            barrier, inc=1, device_id={"mesh": lax.rem(me + step, n_mesh)}, device_id_type=MESH
        )

    @pl.when(has_low)
    def _():
        pl.semaphore_signal(
            barrier, inc=1, device_id={"mesh": me - 1, "harm": other}, device_id_type=MESH
        )

    @pl.when(has_up)
    def _():
        pl.semaphore_signal(
            barrier, inc=1, device_id={"mesh": me + 1, "harm": other}, device_id_type=MESH
        )

    load_copy = pltpu.make_async_copy(load_hbm, load_ref, local_sem.at[0])
    basis_copy = pltpu.make_async_copy(basis_hbm, basis_ref, local_sem.at[1])
    load_copy.start()
    basis_copy.start()

    high, lower = halves(coef_ref[...])
    own_hl[0:rows, :] = high
    own_hl[rows : 2 * rows, :] = lower
    shared = jnp.concatenate([ghost_ref[1:2, :], ghost_ref[0:1, :]], axis=1)
    node_ids = lax.broadcasted_iota(jnp.int32, (nodes, 2 * ghosts), 0)
    pick[...] = jnp.where(node_ids == shared, 1.0, 0.0).astype(BF16)
    picked = dot(own_hl[...], pick[...])
    ghost_out[...] = picked[0:rows] + picked[rows : 2 * rows]

    arrivals = n_mesh + has_low.astype(jnp.int32) + has_up.astype(jnp.int32)
    pl.semaphore_wait(barrier, arrivals)

    coef_copy = pltpu.make_async_remote_copy(
        src_ref=coef_ref, dst_ref=coef_in, send_sem=coef_sem.at[0], recv_sem=coef_sem.at[1],
        device_id={"harm": other}, device_id_type=MESH,
    )
    coef_copy.start()

    def border(src, dst, send_sem, recv_sem, side, rel):
        return pltpu.make_async_remote_copy(
            src_ref=src, dst_ref=dst.at[side, rel], send_sem=send_sem.at[side, rel],
            recv_sem=recv_sem.at[side, rel],
            device_id={
                "mesh": me + 1 if side == 0 else me - 1, "harm": harm if rel == 0 else other,
            },
            device_id_type=MESH,
        )

    there = (has_up, has_low)
    come = (has_low, has_up)

    def border_start(src, dst, send_sem, recv_sem, rel):
        for side in (0, 1):
            @pl.when(there[side])
            def _():
                border(src, dst, send_sem, recv_sem, side, rel).start()

    def border_wait_recv(src, dst, send_sem, recv_sem, rel):
        for side in (0, 1):
            @pl.when(come[side])
            def _():
                border(src, dst, send_sem, recv_sem, side, rel).wait_recv()

            @pl.when(jnp.logical_not(come[side]))
            def _():
                dst[side, rel] = jnp.zeros(dst.shape[2:], F32)

    def border_wait_send(src, dst, send_sem, recv_sem, rel):
        for side in (0, 1):
            @pl.when(there[side])
            def _():
                border(src, dst, send_sem, recv_sem, side, rel).wait_send()

    ghost_args = (ghost_out, ghost_in, ghost_send_sem, ghost_recv_sem)
    border_start(*ghost_args, 0)
    border_start(*ghost_args, 1)

    mine = pl.ds(pl.multiple_of(harm * elems, elems), elems)
    step_rows = 64

    def fill(k, _):
        base = pl.multiple_of(k * step_rows, step_rows)
        for at in range(0, elems, LANES):
            cols = pl.ds(pl.multiple_of(harm * elems + at, LANES), LANES)
            ids = lax.broadcasted_iota(jnp.int32, (step_rows, LANES), 0) + base
            first = jnp.where(ids == conn_ref[0:1, cols], 1.0, 0.0)
            second = jnp.where(ids == conn_ref[1:2, cols], 1.0, 0.0)
            third = jnp.where(ids == conn_ref[2:3, cols], 1.0, 0.0)
            inc[pl.ds(base, step_rows), at : at + LANES] = (second - first).astype(BF16)
            inc[pl.ds(base, step_rows), elems + at : elems + at + LANES] = (third - first).astype(BF16)
        return 0

    lax.fori_loop(0, slots // step_rows, fill, 0)

    row = order_ref[...]
    row = jnp.where(harm == 0, row, jnp.concatenate([row[:, block:], row[:, :block]], axis=1))
    row3 = jnp.concatenate([row, row, row], axis=1)
    synth = wave(row3, lax.broadcasted_iota(jnp.int32, (ncoef, 3 * ncoef), 0), ncoef)
    third_part = lax.broadcasted_iota(jnp.int32, (ncoef, 3 * ncoef), 1) >= 2 * ncoef
    high, lower = halves(synth)
    synth3 = jnp.where(third_part, lower.astype(F32), high.astype(F32)).astype(BF16)
    eye = lax.broadcasted_iota(jnp.int32, (ncoef, ncoef), 0) == lax.broadcasted_iota(
        jnp.int32, (ncoef, ncoef), 1
    )
    column = jnp.sum(jnp.where(eye, row.astype(F32), 0.0), axis=1, keepdims=True).astype(jnp.int32)
    samples = lax.broadcasted_iota(jnp.int32, (ncoef, 3 * ncoef), 1) % ncoef
    weight = jnp.where((column == 0) | (column == ncoef - 1), 1.0, 2.0) / ncoef
    high, lower = halves(wave(column, samples, ncoef) * weight)
    proj3 = jnp.where(third_part, lower.astype(F32), high.astype(F32)).astype(BF16)
    freq = (OMEGA * ((column[0:block] + 1) // 2).astype(F32)) ** 2

    for at in range(0, 2 * elems, LANES):
        edge_own[:, at : at + LANES] = dot(own_hl[...], inc[0:nodes, at : at + LANES])

    coef_copy.wait_recv()
    high, lower = halves(coef_in[...])
    other_hl[0:rows, 0:nodes] = high
    other_hl[rows : 2 * rows, 0:nodes] = lower
    lane = lax.broadcasted_iota(jnp.int32, (rows, 2 * ghosts), 1)
    border_wait_recv(*ghost_args, 0)
    border_wait_recv(*ghost_args, 1)
    high, lower = halves(jnp.where(lane < ghosts, ghost_in[0, 0], ghost_in[1, 0]))
    ghost_hl[0:rows, :] = high
    ghost_hl[rows : 2 * rows, :] = lower
    high, lower = halves(jnp.where(lane < ghosts, ghost_in[0, 1], ghost_in[1, 1]))
    other_hl[0:rows, nodes:slots] = high
    other_hl[rows : 2 * rows, nodes:slots] = lower

    for at in range(0, 2 * elems, LANES):
        cols = slice(at, at + LANES)
        mine_edges = edge_own[:, cols] + dot(ghost_hl[...], inc[nodes:slots, cols])
        other_edges = dot(other_hl[...], inc[:, cols])
        for half, edges in enumerate((mine_edges, other_edges)):
            high, lower = halves(edges[0:rows] + edges[rows : 2 * rows])
            for c in range(3):
                part = slice(c * block, (c + 1) * block)
                for third, piece in enumerate((high, lower, high)):
                    top = third * ncoef + half * block
                    edge_hl[c, top : top + block, cols] = piece[part]
    for c in range(3):
        for at in range(0, 2 * elems, LANES):
            cols = slice(at, at + LANES)
            disp[c, :, cols] = dot(synth3, edge_hl[c, :, cols])

    def sample_rows(k, _):
        base = pl.multiple_of(k * 16, 16)
        times = pl.ds(base, 16)
        for at in range(0, elems, LANES):
            cols = pl.ds(pl.multiple_of(harm * elems + at, LANES), LANES)
            stiff = stiff_ref[0:1, cols]
            refs_b = [edge_ref[c, 0:1, cols] for c in range(3)]
            refs_c = [edge_ref[c, 1:2, cols] for c in range(3)]
            refs_d = [x - y for x, y in zip(refs_c, refs_b)]

            def pull(stretch, refs):
                rest = refs[0] * refs[0] + refs[1] * refs[1] + refs[2] * refs[2]
                square = stretch[0] * stretch[0] + stretch[1] * stretch[1] + stretch[2] * stretch[2]
                return stiff * (0.5 * (square - rest) + PRESTRESS)

            str_b = [refs_b[c] + disp[c, times, at : at + LANES] for c in range(3)]
            str_c = [refs_c[c] + disp[c, times, elems + at : elems + at + LANES] for c in range(3)]
            str_d = [x - y for x, y in zip(str_c, str_b)]
            ten_b = pull(str_b, refs_b)
            ten_c = pull(str_c, refs_c)
            ten_d = pull(str_d, refs_d)
            for c in range(3):
                mid = ten_d * str_d[c]
                for which, value in enumerate((ten_b * str_b[c] - mid, ten_c * str_c[c] + mid)):
                    high, lower = halves(value)
                    to = slice(which * elems + at, which * elems + at + LANES)
                    force_hl[c, times, to] = high
                    force_hl[c, pl.ds(base + ncoef, 16), to] = lower
                    force_hl[c, pl.ds(base + 2 * ncoef, 16), to] = high
        return 0

    lax.fori_loop(0, ncoef // 16, sample_rows, 0)

    for c in range(3):
        for at in range(0, 2 * elems, LANES):
            cols = slice(at, at + LANES)
            value = dot(proj3, force_hl[c, :, cols])
            high, lower = halves(value)
            for half in (0, 1):
                part = slice(half * block, (half + 1) * block)
                coef_hl[half, c * block : (c + 1) * block, cols] = high[part]
                coef_hl[half, rows + c * block : rows + (c + 1) * block, cols] = lower[part]

    def spread(half, start, stop):
        summed = dot_t(coef_hl[half], inc[start:stop, :])
        return summed[0:rows] + summed[rows : 2 * rows]

    back_args = [
        (back_out.at[rel], back_in, back_send_sem, back_recv_sem, rel) for rel in (0, 1)
    ]
    back_out[1] = spread(1, nodes, slots)
    border_start(*back_args[1])
    back_out[0] = spread(0, nodes, slots)
    border_start(*back_args[0])
    for at in range(0, nodes, LANES):
        part_out[:, at : at + LANES] = spread(1, at, at + LANES)
    part_copy = pltpu.make_async_remote_copy(
        src_ref=part_out, dst_ref=part_in, send_sem=part_sem.at[0], recv_sem=part_sem.at[1],
        device_id={"harm": other}, device_id_type=MESH,
    )
    part_copy.start()
    load_copy.wait()
    for at in range(0, nodes, LANES):
        cols = slice(at, at + LANES)
        main_own[:, cols] = spread(0, at, at + LANES)

    border_wait_recv(*back_args[0])
    border_wait_recv(*back_args[1])
    back = jnp.where(lane < ghosts, back_in[1, 0] + back_in[1, 1], back_in[0, 0] + back_in[0, 1])
    high, lower = halves(back)
    ghost_hl[0:rows, :] = high
    ghost_hl[rows : 2 * rows, :] = lower
    part_copy.wait_recv()
    for at in range(0, nodes, LANES):
        cols = slice(at, at + LANES)
        added = dot_t(ghost_hl[...], pick[at : at + LANES, :])
        forces = main_own[:, cols] + part_in[:, cols] + (added[0:rows] + added[rows : 2 * rows])
        for c in range(3):
            part = slice(c * block, (c + 1) * block)
            inertia = freq * mass_ref[0:1, cols] * coef_ref[part, cols]
            value = forces[part] - inertia - load_ref[part, cols]
            resid_ref[part, cols] = value
            low[c, :, cols] = value.astype(BF16)

    basis_copy.wait()
    total = None
    for c in range(3):
        term = dot_t(basis_ref[c], low[c])
        total = term if total is None else total + term
    for piece in range(n_mesh):
        prod_out[piece] = total[piece * share : (piece + 1) * share]

    prod_copies = []
    for step in range(1, n_mesh):
        peer = lax.rem(me + step, n_mesh)
        copy = pltpu.make_async_remote_copy(
            src_ref=prod_out.at[peer], dst_ref=prod_in.at[step - 1],
            send_sem=prod_send_sem.at[step - 1], recv_sem=prod_recv_sem.at[step - 1],
            device_id={"mesh": peer}, device_id_type=MESH,
        )
        copy.start()
        prod_copies.append(copy)

    coef_copy.wait_send()
    part_copy.wait_send()
    for rel in (0, 1):
        border_wait_send(*ghost_args, rel)
        border_wait_send(*back_args[rel])
    for copy in prod_copies:
        copy.wait_recv()
    result = prod_out[me]
    for step in range(1, n_mesh):
        result = result + prod_in[step - 1]
    reduced_ref[...] = result
    for copy in prod_copies:
        copy.wait_send()


def per_device(coeffs, load, mass, stiffness, edge_ref, conn, ghost_send, order, basis):
    n_mesh = lax.axis_size("mesh")
    block, _, nodes = coeffs.shape
    rows = 3 * block
    ncoef = 2 * block
    elems = conn.shape[1] // 2
    ghosts = ghost_send.shape[1]
    slots = nodes + 2 * ghosts
    basis_count = basis.shape[0]
    share = basis_count // n_mesh
    vmem = pl.BlockSpec(memory_space=pltpu.VMEM)
    anywhere = pl.BlockSpec(memory_space=pl.ANY)
    dma = pltpu.SemaphoreType.DMA

    def body(*refs):
        kernel(n_mesh, *refs)

    resid, reduced = pl.pallas_call(
        body,
        out_shape=(
            jax.ShapeDtypeStruct((rows, nodes), F32),
            jax.ShapeDtypeStruct((share, block), F32),
        ),
        in_specs=[vmem, anywhere, vmem, vmem, vmem, vmem, vmem, vmem, anywhere],
        out_specs=(vmem, vmem),
        scratch_shapes=[
            pltpu.VMEM((rows, nodes), F32),
            pltpu.VMEM((3, basis_count, nodes), BF16),
            pltpu.VMEM((rows, nodes), F32),
            pltpu.VMEM((2 * rows, nodes), BF16),
            pltpu.VMEM((2 * rows, slots), BF16),
            pltpu.VMEM((nodes, 2 * ghosts), BF16),
            pltpu.VMEM((slots, 2 * elems), BF16),
            pltpu.VMEM((rows, 2 * ghosts), F32),
            pltpu.VMEM((2, 2, rows, 2 * ghosts), F32),
            pltpu.VMEM((2 * rows, 2 * ghosts), BF16),
            pltpu.VMEM((2 * rows, 2 * elems), F32),
            pltpu.VMEM((3, 3 * ncoef, 2 * elems), BF16),
            pltpu.VMEM((3, ncoef, 2 * elems), F32),
            pltpu.VMEM((3, 3 * ncoef, 2 * elems), BF16),
            pltpu.VMEM((2, 2 * rows, 2 * elems), BF16),
            pltpu.VMEM((2, rows, 2 * ghosts), F32),
            pltpu.VMEM((2, 2, rows, 2 * ghosts), F32),
            pltpu.VMEM((rows, nodes), F32),
            pltpu.VMEM((rows, nodes), F32),
            pltpu.VMEM((rows, nodes), F32),
            pltpu.VMEM((3, block, nodes), BF16),
            pltpu.VMEM((n_mesh, share, block), F32),
            pltpu.VMEM((n_mesh - 1, share, block), F32),
            dma((2,)),
            dma((2,)),
            dma((2, 2)),
            dma((2, 2)),
            dma((2,)),
            dma((2, 2)),
            dma((2, 2)),
            dma((n_mesh - 1,)),
            dma((n_mesh - 1,)),
        ],
        compiler_params=pltpu.CompilerParams(
            collective_id=0, has_side_effects=True, vmem_limit_bytes=48 * 1024 * 1024
        ),
    )(
        coeffs.transpose(1, 0, 2).reshape(rows, nodes),
        load.transpose(1, 0, 2).reshape(rows, nodes),
        mass.reshape(1, -1),
        stiffness.reshape(1, -1),
        edge_ref.transpose(1, 0, 2),
        conn,
        ghost_send,
        order.reshape(1, -1),
        basis.transpose(1, 0, 2),
    )
    return resid.reshape(3, block, nodes).transpose(1, 0, 2), reduced


def solution(mesh):
    in_specs = (
        P("harm", None, ("case", "mesh")),
        P("harm", None, ("case", "mesh")),
        P("mesh"),
        P("mesh"),
        P(None, None, "mesh"),
        P(None, "mesh"),
        P(None, "mesh"),
        P(),
        P(None, None, "mesh"),
    )
    out_specs = (P("harm", None, ("case", "mesh")), P("mesh", ("case", "harm")))
    return jax.shard_map(
        per_device, mesh=mesh, in_specs=in_specs, out_specs=out_specs, check_vma=False
    )
```

time: 131 us -> 35.7 us (0.27)
  blocking collectives: 40 us -> 0 us
  matrix products: 34.6 us -> 0 us
  Pallas kernels: 0 us -> 25.6 us
  waiting for transfers between devices: 17.5 us -> 0 us
  between operations: 14.3 us -> 0.66 us
  starting transfers between devices: 11.7 us -> 0 us
  other arithmetic: 3.74 us -> 0 us
    psum x1 -> x0, blocking collectives: 37.3 us -> none  [per_device(): summed_proj = lax.psum(partial_proj, 'mesh')]
    dot_general x11 -> x0, matrix products: 34.6 us -> none  [the longest x4 20.6 us: spread_rows(): lax.dot_general(flat, table, (((1,), (1,)), ((), ())), precision=lax.Prec...]
    pallas_call x0 -> x1, Pallas kernels: none -> 25.6 us  [per_device(): pl.pallas_call(body, out_shape=(jax.ShapeDtypeStruct((rows, nodes), F32),...]
    ppermute x4 -> x0, starting transfers between devices: 11.7 us -> none  [the longest x2 9.11 us: extended_2(): before = lax.ppermute(last, axis, up)]
    ppermute x4 -> x0, waiting for transfers between devices: 8.98 us -> none  [the longest x2 8.52 us: extended_2(): after = lax.ppermute(first, axis, down)]
    reduce_scatter x1 -> x0, waiting for transfers between devices: 8.48 us -> none  [per_device(): lax.psum_scatter(jnp.dot(proj_mine, flat_forces, precision=lax.Precision....]
    unnamed x22 -> x20, local copies, waits for them, and re-layouts: 1.76 us -> 9.02 us
    reshape x6 -> x0, local copies, waits for them, and re-layouts: 4.45 us -> none  [the longest x1 1.28 us: internal_forces(): on_third = (force_ac + force_bc).reshape(time_rows * 3, elem_count)]
  transfers between devices with their start and end apart: 5 -> 0, of which waited for: 5 -> 0; matrix products, arithmetic and copies ran while one was open for 0% -> 0% of each run, Pallas kernels for 0% -> 0%
where the time goes in v1:
time: 35.7 us; the launch traced here: 35.2 us
  Pallas kernels  25.6 us (72%)
  local copies, waits for them, and re-layouts  9.02 us (25%)
  between operations  0.66 us (2%)
    pallas_call x1, Pallas kernels, per_device(): pl.pallas_call(body, out_shape=(jax.ShapeDtypeStruct((rows, nodes), F32),...  25.6 us
    unnamed x20, local copies, waits for them, and re-layouts  9.02 us

profile of v1, /device:TPU:0, one launch (start us, length us, event | category | flops | bytes accessed | tf_op | source)
XLA Modules:
  0.0 35.2 jit_solution(4411667789900185924)
XLA Ops:
  0.6 0.0 copy-start
  0.6 1.4 %copy-done = bf16[256,3,1024]{2,0,1:T(8,128)(2,1)S(1)} copy-done((bf16[256,3,1024]{2,0,1:T(8,128)(2,1)S(1)}, bf16[256,3,1024]{2,0,1:T(8,128)(2,1)}, u32[]{:S(2)}) %copy-start) | copy-done | bytes 1572888
  2.0 0.0 copy-start.1
  2.0 1.0 %copy-done.1 = f32[32,3,1024]{2,0,1:T(8,128)S(1)} copy-done((f32[32,3,1024]{2,0,1:T(8,128)S(1)}, f32[32,3,1024]{2,0,1:T(8,128)}, u32[]{:S(2)}) %copy-start.1) | copy-done | bytes 393240
  3.0 0.0 copy-start.2
  3.0 1.0 %copy-done.2 = f32[32,3,1024]{2,0,1:T(8,128)S(1)} copy-done((f32[32,3,1024]{2,0,1:T(8,128)S(1)}, f32[32,3,1024]{2,0,1:T(8,128)}, u32[]{:S(2)}) %copy-start.2) | copy-done | bytes 393240
  4.0 0.0 copy-start.3
  4.0 0.8 %copy-done.3 = f32[2,3,2048]{2,0,1:T(2,128)S(1)} copy-done((f32[2,3,2048]{2,0,1:T(2,128)S(1)}, f32[2,3,2048]{2,0,1:T(2,128)}, u32[]{:S(2)}) %copy-start.3) | copy-done | bytes 49176
  4.8 0.0 copy-start.4
  4.8 0.8 %copy-done.4 = s32[3,2048]{1,0:T(4,128)S(1)} copy-done((s32[3,2048]{1,0:T(4,128)S(1)}, s32[3,2048]{1,0:T(4,128)}, u32[]{:S(2)}) %copy-start.4) | copy-done | bytes 24600
  5.6 0.0 copy-start.5
  5.6 0.7 %copy-done.5 = f32[2048]{0:T(1024)S(1)} copy-done((f32[2048]{0:T(1024)S(1)}, f32[2048]{0:T(1024)}, u32[]{:S(2)}) %copy-start.5) | copy-done | bytes 8216
  6.3 0.0 copy-start.6
  6.3 0.7 %copy-done.6 = f32[1024]{0:T(1024)S(1)} copy-done((f32[1024]{0:T(1024)S(1)}, f32[1024]{0:T(1024)}, u32[]{:S(2)}) %copy-start.6) | copy-done | bytes 4120
  7.0 0.0 copy-start.7
  7.0 0.7 %copy-done.7 = s32[2,64]{1,0:T(2,128)S(1)} copy-done((s32[2,64]{1,0:T(2,128)S(1)}, s32[2,64]{1,0:T(2,128)}, u32[]{:S(2)}) %copy-start.7) | copy-done | bytes 536
  7.7 0.0 copy-start.8
  7.7 0.7 %copy-done.8 = s32[64]{0:T(128)S(1)} copy-done((s32[64]{0:T(128)S(1)}, s32[64]{0:T(128)}, u32[]{:S(2)}) %copy-start.8) | copy-done | bytes 280
  8.3 25.6 %shard_map.104 = (f32[96,1024]{1,0:T(8,128)S(1)}, f32[32,32]{1,0:T(8,128)S(1)}) custom-call(f32[96,1024]{1,0:T(8,128)S(1)} %bitcast.15, f32[96,1024]{1,0:T(8,128)S(1)} %bitcast.16, f32[1,1024]{1,0:T(1,128)S(1)} %bitcast.20, f32[1,2048]{1,0:T(1,128)S(1)} %bitcast.19, f32[3,2,2048]{2,1,0:T(2,128)S(1)} %bitcast.18, s32[3,2048]{1,0:T(4,128)S(1)} %copy-done.4, ...), custom_call_target="tpu_custom_call" | custom-call | tf_op jit(solution)/shard_map/pallas_call | solution.py:344
  33.9 0.7 %copy.13 = f32[32,3,1024]{2,0,1:T(8,128)} copy(f32[32,3,1024]{2,0,1:T(8,128)S(1)} %bitcast.17) | data formatting | bytes 786432
  34.6 0.6 %copy.14 = f32[32,32]{1,0:T(8,128)} copy(f32[32,32]{1,0:T(8,128)S(1)} %get-tuple-element.9) | data formatting | bytes 8192
Async XLA Ops:
  0.6 1.4 %copy-start = (bf16[256,3,1024]{2,0,1:T(8,128)(2,1)S(1)}, bf16[256,3,1024]{2,0,1:T(8,128)(2,1)}, u32[]{:S(2)}) copy-start(bf16[256,3,1024]{2,0,1:T(8,128)(2,1)} %param.17) | copy-start | bytes 4718596
  2.0 1.0 %copy-start.1 = (f32[32,3,1024]{2,0,1:T(8,128)S(1)}, f32[32,3,1024]{2,0,1:T(8,128)}, u32[]{:S(2)}) copy-start(f32[32,3,1024]{2,0,1:T(8,128)} %param.9) | copy-start | bytes 1179652
  3.0 1.0 %copy-start.2 = (f32[32,3,1024]{2,0,1:T(8,128)S(1)}, f32[32,3,1024]{2,0,1:T(8,128)}, u32[]{:S(2)}) copy-start(f32[32,3,1024]{2,0,1:T(8,128)} %param.10) | copy-start | bytes 1179652
  4.0 0.8 %copy-start.3 = (f32[2,3,2048]{2,0,1:T(2,128)S(1)}, f32[2,3,2048]{2,0,1:T(2,128)}, u32[]{:S(2)}) copy-start(f32[2,3,2048]{2,0,1:T(2,128)} %param.13) | copy-start | bytes 147460
  4.8 0.8 %copy-start.4 = (s32[3,2048]{1,0:T(4,128)S(1)}, s32[3,2048]{1,0:T(4,128)}, u32[]{:S(2)}) copy-start(s32[3,2048]{1,0:T(4,128)} %refs_5_.1) | copy-start | bytes 73732
  5.6 0.7 %copy-start.5 = (f32[2048]{0:T(1024)S(1)}, f32[2048]{0:T(1024)}, u32[]{:S(2)}) copy-start(f32[2048]{0:T(1024)} %param.12) | copy-start | bytes 24580
  6.3 0.7 %copy-start.6 = (f32[1024]{0:T(1024)S(1)}, f32[1024]{0:T(1024)}, u32[]{:S(2)}) copy-start(f32[1024]{0:T(1024)} %param.11) | copy-start | bytes 12292
  7.0 0.7 %copy-start.7 = (s32[2,64]{1,0:T(2,128)S(1)}, s32[2,64]{1,0:T(2,128)}, u32[]{:S(2)}) copy-start(s32[2,64]{1,0:T(2,128)} %refs_6_.1) | copy-start | bytes 1540
  7.7 0.7 %copy-start.8 = (s32[64]{0:T(128)S(1)}, s32[64]{0:T(128)}, u32[]{:S(2)}) copy-start(s32[64]{0:T(128)} %param.16) | copy-start | bytes 772

commit v2 on v1

--- a/solution.py
+++ b/solution.py
@@ -30,17 +30,43 @@
 
 def wave(order, samples, ncoef):
     harmonic = (order + 1) // 2
-    phase = (harmonic * samples) % ncoef
-    angle = (2.0 * math.pi / ncoef) * phase.astype(F32)
     cosine = (order % 2 == 1) | (order == 0)
-    return jnp.where(cosine, jnp.cos(angle), jnp.sin(angle))
+    phase = harmonic * samples + jnp.where(cosine, 0, ncoef - ncoef // 4)
+    phase = (phase + ncoef // 2) % ncoef - ncoef // 2
+    return jnp.cos((2.0 * math.pi / ncoef) * phase.astype(F32))
+
+
+def in_three(table):
+    high, lower = halves(table)
+    high = high.astype(F32)
+    return jnp.concatenate([high, high, lower.astype(F32)], axis=1).astype(BF16)
+
+
+def pack_border(full):
+    rows, lanes = full.shape
+    first = lax.broadcasted_iota(jnp.int32, (rows // 2, lanes), 1) < lanes // 2
+    turned = pltpu.roll(full, lanes // 2, 1)
+    half = rows // 2
+    return (
+        jnp.where(first, full[:half], turned[half:]),
+        jnp.where(first, turned[:half], full[half:]),
+    )
+
+
+def unpack_border(low_part, high_part):
+    half, lanes = low_part.shape
+    first = lax.broadcasted_iota(jnp.int32, (half, lanes), 1) < lanes // 2
+    top = jnp.where(first, low_part, pltpu.roll(high_part, lanes // 2, 1))
+    bottom = jnp.where(first, pltpu.roll(low_part, lanes // 2, 1), high_part)
+    return jnp.concatenate([top, bottom], axis=0)
 
 
 def kernel(
     n_mesh,
-    coef_ref, load_hbm, mass_ref, stiff_ref, edge_ref, conn_ref, ghost_ref, order_ref, basis_hbm,
+    coef_hbm, load_hbm, mass_hbm, stiff_hbm, edge_hbm, conn_hbm, ghost_hbm, order_hbm, basis_hbm,
     resid_ref, reduced_ref,
-    load_ref, basis_ref, coef_in, own_hl, other_hl, pick, inc, ghost_out, ghost_in, ghost_hl,
+    coef_ref, load_ref, mass_ref, stiff_ref, edge_ref, conn_ref, ghost_ref, order_ref, basis_ref,
+    coef_in, own_hl, other_hl, pick, inc, ghost_out, ghost_in, ghost_hl,
     edge_own, edge_hl, disp, force_hl, coef_hl, back_out, back_in, part_out, part_in, main_own, low,
     prod_out, prod_in,
     local_sem, coef_sem, ghost_send_sem, ghost_recv_sem, part_sem,
@@ -52,7 +78,9 @@
     ghosts = ghost_ref.shape[1]
     elems = conn_ref.shape[1] // 2
     slots = nodes + 2 * ghosts
-    share = prod_out.shape[1]
+    sub = prod_out.shape[1]
+    fold = prod_out.shape[2] // block
+    share = sub * fold
     me = lax.axis_index("mesh")
     harm = lax.axis_index("harm")
     other = 1 - harm
@@ -77,10 +105,17 @@
             barrier, inc=1, device_id={"mesh": me + 1, "harm": other}, device_id_type=MESH
         )
 
-    load_copy = pltpu.make_async_copy(load_hbm, load_ref, local_sem.at[0])
-    basis_copy = pltpu.make_async_copy(basis_hbm, basis_ref, local_sem.at[1])
-    load_copy.start()
-    basis_copy.start()
+    fetch = {}
+    for at, (name, src, dst) in enumerate((
+        ("coef", coef_hbm, coef_ref), ("ghost", ghost_hbm, ghost_ref), ("conn", conn_hbm, conn_ref),
+        ("order", order_hbm, order_ref), ("edge", edge_hbm, edge_ref),
+        ("stiff", stiff_hbm, stiff_ref), ("mass", mass_hbm, mass_ref),
+        ("load", load_hbm, load_ref), ("basis", basis_hbm, basis_ref),
+    )):
+        fetch[name] = pltpu.make_async_copy(src, dst, local_sem.at[at])
+        fetch[name].start()
+    fetch["coef"].wait()
+    fetch["ghost"].wait()
 
     high, lower = halves(coef_ref[...])
     own_hl[0:rows, :] = high
@@ -89,7 +124,7 @@
     node_ids = lax.broadcasted_iota(jnp.int32, (nodes, 2 * ghosts), 0)
     pick[...] = jnp.where(node_ids == shared, 1.0, 0.0).astype(BF16)
     picked = dot(own_hl[...], pick[...])
-    ghost_out[...] = picked[0:rows] + picked[rows : 2 * rows]
+    ghost_out[0], ghost_out[1] = pack_border(picked[0:rows] + picked[rows : 2 * rows])
 
     arrivals = n_mesh + has_low.astype(jnp.int32) + has_up.astype(jnp.int32)
     pl.semaphore_wait(barrier, arrivals)
@@ -102,7 +137,7 @@
 
     def border(src, dst, send_sem, recv_sem, side, rel):
         return pltpu.make_async_remote_copy(
-            src_ref=src, dst_ref=dst.at[side, rel], send_sem=send_sem.at[side, rel],
+            src_ref=src.at[side], dst_ref=dst.at[side, rel], send_sem=send_sem.at[side, rel],
             recv_sem=recv_sem.at[side, rel],
             device_id={
                 "mesh": me + 1 if side == 0 else me - 1, "harm": harm if rel == 0 else other,
@@ -138,6 +173,8 @@
     ghost_args = (ghost_out, ghost_in, ghost_send_sem, ghost_recv_sem)
     border_start(*ghost_args, 0)
     border_start(*ghost_args, 1)
+
+    fetch["conn"].wait()
 
     mine = pl.ds(pl.multiple_of(harm * elems, elems), elems)
     step_rows = 64
@@ -156,21 +193,16 @@
 
     lax.fori_loop(0, slots // step_rows, fill, 0)
 
+    fetch["order"].wait()
     row = order_ref[...]
     row = jnp.where(harm == 0, row, jnp.concatenate([row[:, block:], row[:, :block]], axis=1))
-    row3 = jnp.concatenate([row, row, row], axis=1)
-    synth = wave(row3, lax.broadcasted_iota(jnp.int32, (ncoef, 3 * ncoef), 0), ncoef)
-    third_part = lax.broadcasted_iota(jnp.int32, (ncoef, 3 * ncoef), 1) >= 2 * ncoef
-    high, lower = halves(synth)
-    synth3 = jnp.where(third_part, lower.astype(F32), high.astype(F32)).astype(BF16)
-    eye = lax.broadcasted_iota(jnp.int32, (ncoef, ncoef), 0) == lax.broadcasted_iota(
-        jnp.int32, (ncoef, ncoef), 1
-    )
-    column = jnp.sum(jnp.where(eye, row.astype(F32), 0.0), axis=1, keepdims=True).astype(jnp.int32)
-    samples = lax.broadcasted_iota(jnp.int32, (ncoef, 3 * ncoef), 1) % ncoef
+    lanes = lax.broadcasted_iota(jnp.int32, (ncoef, ncoef), 1)
+    subs = lax.broadcasted_iota(jnp.int32, (ncoef, ncoef), 0)
+    synth3 = in_three(wave(row, subs, ncoef))
+    column = jnp.sum(jnp.where(lanes == subs, row.astype(F32), 0.0), axis=1, keepdims=True)
+    column = column.astype(jnp.int32)
     weight = jnp.where((column == 0) | (column == ncoef - 1), 1.0, 2.0) / ncoef
-    high, lower = halves(wave(column, samples, ncoef) * weight)
-    proj3 = jnp.where(third_part, lower.astype(F32), high.astype(F32)).astype(BF16)
+    proj3 = in_three(wave(column, lanes, ncoef) * weight)
     freq = (OMEGA * ((column[0:block] + 1) // 2).astype(F32)) ** 2
 
     for at in range(0, 2 * elems, LANES):
@@ -180,13 +212,12 @@
     high, lower = halves(coef_in[...])
     other_hl[0:rows, 0:nodes] = high
     other_hl[rows : 2 * rows, 0:nodes] = lower
-    lane = lax.broadcasted_iota(jnp.int32, (rows, 2 * ghosts), 1)
     border_wait_recv(*ghost_args, 0)
     border_wait_recv(*ghost_args, 1)
-    high, lower = halves(jnp.where(lane < ghosts, ghost_in[0, 0], ghost_in[1, 0]))
+    high, lower = halves(unpack_border(ghost_in[0, 0], ghost_in[1, 0]))
     ghost_hl[0:rows, :] = high
     ghost_hl[rows : 2 * rows, :] = lower
-    high, lower = halves(jnp.where(lane < ghosts, ghost_in[0, 1], ghost_in[1, 1]))
+    high, lower = halves(unpack_border(ghost_in[0, 1], ghost_in[1, 1]))
     other_hl[0:rows, nodes:slots] = high
     other_hl[rows : 2 * rows, nodes:slots] = lower
 
@@ -206,6 +237,8 @@
             cols = slice(at, at + LANES)
             disp[c, :, cols] = dot(synth3, edge_hl[c, :, cols])
 
+    fetch["edge"].wait()
+    fetch["stiff"].wait()
     def sample_rows(k, _):
         base = pl.multiple_of(k * 16, 16)
         times = pl.ds(base, 16)
@@ -256,9 +289,9 @@
     back_args = [
         (back_out.at[rel], back_in, back_send_sem, back_recv_sem, rel) for rel in (0, 1)
     ]
-    back_out[1] = spread(1, nodes, slots)
+    back_out[1, 1], back_out[1, 0] = pack_border(spread(1, nodes, slots))
     border_start(*back_args[1])
-    back_out[0] = spread(0, nodes, slots)
+    back_out[0, 1], back_out[0, 0] = pack_border(spread(0, nodes, slots))
     border_start(*back_args[0])
     for at in range(0, nodes, LANES):
         part_out[:, at : at + LANES] = spread(1, at, at + LANES)
@@ -267,14 +300,15 @@
         device_id={"harm": other}, device_id_type=MESH,
     )
     part_copy.start()
-    load_copy.wait()
+    fetch["load"].wait()
+    fetch["mass"].wait()
     for at in range(0, nodes, LANES):
         cols = slice(at, at + LANES)
         main_own[:, cols] = spread(0, at, at + LANES)
 
     border_wait_recv(*back_args[0])
     border_wait_recv(*back_args[1])
-    back = jnp.where(lane < ghosts, back_in[1, 0] + back_in[1, 1], back_in[0, 0] + back_in[0, 1])
+    back = unpack_border(back_in[1, 0] + back_in[1, 1], back_in[0, 0] + back_in[0, 1])
     high, lower = halves(back)
     ghost_hl[0:rows, :] = high
     ghost_hl[rows : 2 * rows, :] = lower
@@ -290,13 +324,15 @@
             resid_ref[part, cols] = value
             low[c, :, cols] = value.astype(BF16)
 
-    basis_copy.wait()
+    fetch["basis"].wait()
     total = None
     for c in range(3):
         term = dot_t(basis_ref[c], low[c])
         total = term if total is None else total + term
     for piece in range(n_mesh):
-        prod_out[piece] = total[piece * share : (piece + 1) * share]
+        prod_out[piece] = jnp.concatenate(
+            [total[piece * share + q * sub : piece * share + (q + 1) * sub] for q in range(fold)], axis=1
+        )
 
     prod_copies = []
     for step in range(1, n_mesh):
@@ -319,7 +355,8 @@
     result = prod_out[me]
     for step in range(1, n_mesh):
         result = result + prod_in[step - 1]
-    reduced_ref[...] = result
+    for q in range(fold):
+        reduced_ref[q * sub : (q + 1) * sub, :] = result[:, q * block : (q + 1) * block]
     for copy in prod_copies:
         copy.wait_send()
 
@@ -334,8 +371,9 @@
     slots = nodes + 2 * ghosts
     basis_count = basis.shape[0]
     share = basis_count // n_mesh
+    fold = min(128 // block, share)
     vmem = pl.BlockSpec(memory_space=pltpu.VMEM)
-    anywhere = pl.BlockSpec(memory_space=pl.ANY)
+    hbm = pl.BlockSpec(memory_space=pltpu.HBM)
     dma = pltpu.SemaphoreType.DMA
 
     def body(*refs):
@@ -347,33 +385,40 @@
             jax.ShapeDtypeStruct((rows, nodes), F32),
             jax.ShapeDtypeStruct((share, block), F32),
         ),
-        in_specs=[vmem, anywhere, vmem, vmem, vmem, vmem, vmem, vmem, anywhere],
+        in_specs=[hbm] * 9,
         out_specs=(vmem, vmem),
         scratch_shapes=[
             pltpu.VMEM((rows, nodes), F32),
+            pltpu.VMEM((rows, nodes), F32),
+            pltpu.VMEM((1, nodes), F32),
+            pltpu.VMEM((1, 2 * elems), F32),
+            pltpu.VMEM((3, 2, 2 * elems), F32),
+            pltpu.VMEM((3, 2 * elems), jnp.int32),
+            pltpu.VMEM((2, ghosts), jnp.int32),
+            pltpu.VMEM((1, ncoef), jnp.int32),
             pltpu.VMEM((3, basis_count, nodes), BF16),
             pltpu.VMEM((rows, nodes), F32),
             pltpu.VMEM((2 * rows, nodes), BF16),
             pltpu.VMEM((2 * rows, slots), BF16),
             pltpu.VMEM((nodes, 2 * ghosts), BF16),
             pltpu.VMEM((slots, 2 * elems), BF16),
-            pltpu.VMEM((rows, 2 * ghosts), F32),
-            pltpu.VMEM((2, 2, rows, 2 * ghosts), F32),
+            pltpu.VMEM((2, rows // 2, 2 * ghosts), F32),
+            pltpu.VMEM((2, 2, rows // 2, 2 * ghosts), F32),
             pltpu.VMEM((2 * rows, 2 * ghosts), BF16),
             pltpu.VMEM((2 * rows, 2 * elems), F32),
             pltpu.VMEM((3, 3 * ncoef, 2 * elems), BF16),
             pltpu.VMEM((3, ncoef, 2 * elems), F32),
             pltpu.VMEM((3, 3 * ncoef, 2 * elems), BF16),
             pltpu.VMEM((2, 2 * rows, 2 * elems), BF16),
-            pltpu.VMEM((2, rows, 2 * ghosts), F32),
-            pltpu.VMEM((2, 2, rows, 2 * ghosts), F32),
+            pltpu.VMEM((2, 2, rows // 2, 2 * ghosts), F32),
+            pltpu.VMEM((2, 2, rows // 2, 2 * ghosts), F32),
             pltpu.VMEM((rows, nodes), F32),
             pltpu.VMEM((rows, nodes), F32),
             pltpu.VMEM((rows, nodes), F32),
             pltpu.VMEM((3, block, nodes), BF16),
-            pltpu.VMEM((n_mesh, share, block), F32),
-            pltpu.VMEM((n_mesh - 1, share, block), F32),
-            dma((2,)),
+            pltpu.VMEM((n_mesh, share // fold, fold * block), F32),
+            pltpu.VMEM((n_mesh - 1, share // fold, fold * block), F32),
+            dma((9,)),
             dma((2,)),
             dma((2, 2)),
             dma((2, 2)),
@@ -384,7 +429,7 @@
             dma((n_mesh - 1,)),
         ],
         compiler_params=pltpu.CompilerParams(
-            collective_id=0, has_side_effects=True, vmem_limit_bytes=48 * 1024 * 1024
+            collective_id=0, has_side_effects=True, vmem_limit_bytes=60 * 1024 * 1024
         ),
     )(
         coeffs.transpose(1, 0, 2).reshape(rows, nodes),

time: 35.7 us -> 26.6 us (0.75)
  local copies, waits for them, and re-layouts: 9.02 us -> 3.09 us
  Pallas kernels: 25.6 us -> 22.7 us
    unnamed x20 -> x2, local copies, waits for them, and re-layouts: 9.02 us -> 3.09 us
    pallas_call x1, Pallas kernels: 25.6 us -> 22.7 us  [per_device(): pl.pallas_call(body, out_shape=(jax.ShapeDtypeStruct((rows, nodes), F32),...]
where the time goes in v2:
time: 26.6 us; the launch traced here: 26.4 us
  Pallas kernels  22.7 us (85%)
  local copies, waits for them, and re-layouts  3.09 us (12%)
  between operations  0.64 us (2%)
    pallas_call x1, Pallas kernels, per_device(): pl.pallas_call(body, out_shape=(jax.ShapeDtypeStruct((rows, nodes), F32),...  22.7 us
    unnamed x2, local copies, waits for them, and re-layouts  3.09 us

profile of v2, /device:TPU:0, one launch (start us, length us, event | category | flops | bytes accessed | tf_op | source)
XLA Modules:
  0.0 26.4 jit_solution(11910002082814496072)
XLA Ops:
  0.6 22.7 %shard_map.104 = (f32[96,1024]{1,0:T(8,128)}, f32[32,32]{1,0:T(8,128)}) custom-call(f32[96,1024]{1,0:T(8,128)} %bitcast.15, f32[96,1024]{1,0:T(8,128)} %bitcast.16, f32[1,1024]{1,0:T(1,128)} %bitcast.20, f32[1,2048]{1,0:T(1,128)} %bitcast.19, f32[3,2,2048]{2,1,0:T(2,128)} %bitcast.18, s32[3,2048]{1,0:T(4,128)} %refs_5_.1, s32[2,64]{1,0:T(2,128)} %refs_6_.1, ...), custom_call_target="tpu_custom_call" | custom-call | tf_op jit(solution)/shard_map/pallas_call | solution.py:382
  23.3 1.8 %copy.13 = f32[32,3,1024]{2,0,1:T(8,128)} copy(f32[32,3,1024]{2,0,1:T(8,128)} %bitcast.17) | data formatting | bytes 786432
  25.1 1.3 %copy.14 = f32[32,32]{1,0:T(8,128)} copy(f32[32,32]{1,0:T(8,128)} %get-tuple-element.9) | data formatting | bytes 8192

commit v3 on v2

--- a/solution.py
+++ b/solution.py
@@ -70,7 +70,7 @@
     edge_own, edge_hl, disp, force_hl, coef_hl, back_out, back_in, part_out, part_in, main_own, low,
     prod_out, prod_in,
     local_sem, coef_sem, ghost_send_sem, ghost_recv_sem, part_sem,
-    back_send_sem, back_recv_sem, prod_send_sem, prod_recv_sem,
+    back_send_sem, back_recv_sem, prod_send_sem, prod_recv_sem, reach_sem,
 ):
     rows, nodes = coef_ref.shape
     block = rows // 3
@@ -88,22 +88,13 @@
 
     barrier = pltpu.get_barrier_semaphore()
     pl.semaphore_signal(barrier, inc=1, device_id={"harm": other}, device_id_type=MESH)
-    for step in range(1, n_mesh):
-        pl.semaphore_signal(
-            barrier, inc=1, device_id={"mesh": lax.rem(me + step, n_mesh)}, device_id_type=MESH
-        )
-
-    @pl.when(has_low)
-    def _():
-        pl.semaphore_signal(
-            barrier, inc=1, device_id={"mesh": me - 1, "harm": other}, device_id_type=MESH
-        )
-
-    @pl.when(has_up)
-    def _():
-        pl.semaphore_signal(
-            barrier, inc=1, device_id={"mesh": me + 1, "harm": other}, device_id_type=MESH
-        )
+    for side_ok, to in ((has_low, me - 1), (has_up, me + 1)):
+        @pl.when(side_ok)
+        def _():
+            for core in (harm, other):
+                pl.semaphore_signal(
+                    barrier, inc=1, device_id={"mesh": to, "harm": core}, device_id_type=MESH
+                )
 
     fetch = {}
     for at, (name, src, dst) in enumerate((
@@ -126,7 +117,7 @@
     picked = dot(own_hl[...], pick[...])
     ghost_out[0], ghost_out[1] = pack_border(picked[0:rows] + picked[rows : 2 * rows])
 
-    arrivals = n_mesh + has_low.astype(jnp.int32) + has_up.astype(jnp.int32)
+    arrivals = 1 + 2 * (has_low.astype(jnp.int32) + has_up.astype(jnp.int32))
     pl.semaphore_wait(barrier, arrivals)
 
     coef_copy = pltpu.make_async_remote_copy(
@@ -144,6 +135,27 @@
             },
             device_id_type=MESH,
         )
+
+    reaches = []
+    while 2 << len(reaches) < n_mesh:
+        reaches.append(2 << len(reaches))
+
+    def tell(at):
+        reach = reaches[at]
+        for ok, to in ((me >= reach, me - reach), (me + reach < n_mesh, me + reach)):
+            @pl.when(ok)
+            def _():
+                pl.semaphore_signal(
+                    reach_sem.at[at], inc=1, device_id={"mesh": to}, device_id_type=MESH
+                )
+
+    def hear(at):
+        reach = reaches[at]
+        count = (me >= reach).astype(jnp.int32) + (me + reach < n_mesh).astype(jnp.int32)
+
+        @pl.when(count > 0)
+        def _():
+            pl.semaphore_wait(reach_sem.at[at], count)
 
     there = (has_up, has_low)
     come = (has_low, has_up)
@@ -214,6 +226,8 @@
     other_hl[rows : 2 * rows, 0:nodes] = lower
     border_wait_recv(*ghost_args, 0)
     border_wait_recv(*ghost_args, 1)
+    if reaches:
+        tell(0)
     high, lower = halves(unpack_border(ghost_in[0, 0], ghost_in[1, 0]))
     ghost_hl[0:rows, :] = high
     ghost_hl[rows : 2 * rows, :] = lower
@@ -236,6 +250,11 @@
         for at in range(0, 2 * elems, LANES):
             cols = slice(at, at + LANES)
             disp[c, :, cols] = dot(synth3, edge_hl[c, :, cols])
+
+    if reaches:
+        hear(0)
+    for at in range(1, min(2, len(reaches))):
+        tell(at)
 
     fetch["edge"].wait()
     fetch["stiff"].wait()
@@ -334,6 +353,10 @@
             [total[piece * share + q * sub : piece * share + (q + 1) * sub] for q in range(fold)], axis=1
         )
 
+    for at in range(1, len(reaches)):
+        hear(at)
+        if at + 1 < len(reaches):
+            tell(at + 1)
     prod_copies = []
     for step in range(1, n_mesh):
         peer = lax.rem(me + step, n_mesh)
@@ -427,6 +450,7 @@
             dma((2, 2)),
             dma((n_mesh - 1,)),
             dma((n_mesh - 1,)),
+            pltpu.SemaphoreType.REGULAR((8,)),
         ],
         compiler_params=pltpu.CompilerParams(
             collective_id=0, has_side_effects=True, vmem_limit_bytes=60 * 1024 * 1024

time: 26.6 us -> 26.8 us (level)
  no operation moved by 1% of the time
where the time goes in v3:
time: 26.8 us; the launch traced here: 26.6 us
  Pallas kernels  22.8 us (85%)
  local copies, waits for them, and re-layouts  3.09 us (12%)
  between operations  0.64 us (2%)
    pallas_call x1, Pallas kernels, per_device(): pl.pallas_call(body, out_shape=(jax.ShapeDtypeStruct((rows, nodes), F32),...  22.8 us
    unnamed x2, local copies, waits for them, and re-layouts  3.09 us

profile of v3, /device:TPU:0, one launch (start us, length us, event | category | flops | bytes accessed | tf_op | source)
XLA Modules:
  0.0 26.6 jit_solution(4657087708196879849)
XLA Ops:
  0.6 22.8 %shard_map.104 = (f32[96,1024]{1,0:T(8,128)}, f32[32,32]{1,0:T(8,128)}) custom-call(f32[96,1024]{1,0:T(8,128)} %bitcast.15, f32[96,1024]{1,0:T(8,128)} %bitcast.16, f32[1,1024]{1,0:T(1,128)} %bitcast.20, f32[1,2048]{1,0:T(1,128)} %bitcast.19, f32[3,2,2048]{2,1,0:T(2,128)} %bitcast.18, s32[3,2048]{1,0:T(4,128)} %refs_5_.1, s32[2,64]{1,0:T(2,128)} %refs_6_.1, ...), custom_call_target="tpu_custom_call" | custom-call | tf_op jit(solution)/shard_map/pallas_call | solution.py:405
  23.5 1.8 %copy.13 = f32[32,3,1024]{2,0,1:T(8,128)} copy(f32[32,3,1024]{2,0,1:T(8,128)} %bitcast.17) | data formatting | bytes 786432
  25.3 1.3 %copy.14 = f32[32,32]{1,0:T(8,128)} copy(f32[32,32]{1,0:T(8,128)} %get-tuple-element.9) | data formatting | bytes 8192

commit v4 on v2

--- a/solution.py
+++ b/solution.py
@@ -304,7 +304,12 @@
     fetch["mass"].wait()
     for at in range(0, nodes, LANES):
         cols = slice(at, at + LANES)
-        main_own[:, cols] = spread(0, at, at + LANES)
+        forces = spread(0, at, at + LANES)
+        for c in range(3):
+            part = slice(c * block, (c + 1) * block)
+            inertia = freq * mass_ref[0:1, cols] * coef_ref[part, cols]
+            main_own[part, cols] = forces[part] - inertia - load_ref[part, cols]
+    fetch["basis"].wait()
 
     border_wait_recv(*back_args[0])
     border_wait_recv(*back_args[1])
@@ -319,12 +324,10 @@
         forces = main_own[:, cols] + part_in[:, cols] + (added[0:rows] + added[rows : 2 * rows])
         for c in range(3):
             part = slice(c * block, (c + 1) * block)
-            inertia = freq * mass_ref[0:1, cols] * coef_ref[part, cols]
-            value = forces[part] - inertia - load_ref[part, cols]
+            value = forces[part]
             resid_ref[part, cols] = value
             low[c, :, cols] = value.astype(BF16)
 
-    fetch["basis"].wait()
     total = None
     for c in range(3):
         term = dot_t(basis_ref[c], low[c])

time: 26.6 us -> 26.6 us (level)
  no operation moved by 1% of the time
where the time goes in v4:
time: 26.6 us; the launch traced here: 26.3 us
  Pallas kernels  22.6 us (85%)
  local copies, waits for them, and re-layouts  3.09 us (12%)
  between operations  0.64 us (2%)
    pallas_call x1, Pallas kernels, per_device(): pl.pallas_call(body, out_shape=(jax.ShapeDtypeStruct((rows, nodes), F32),...  22.6 us
    unnamed x2, local copies, waits for them, and re-layouts  3.09 us

profile of v4, /device:TPU:0, one launch (start us, length us, event | category | flops | bytes accessed | tf_op | source)
XLA Modules:
  0.0 26.3 jit_solution(5123743265092747671)
XLA Ops:
  0.6 22.6 %shard_map.104 = (f32[96,1024]{1,0:T(8,128)}, f32[32,32]{1,0:T(8,128)}) custom-call(f32[96,1024]{1,0:T(8,128)} %bitcast.15, f32[96,1024]{1,0:T(8,128)} %bitcast.16, f32[1,1024]{1,0:T(1,128)} %bitcast.20, f32[1,2048]{1,0:T(1,128)} %bitcast.19, f32[3,2,2048]{2,1,0:T(2,128)} %bitcast.18, s32[3,2048]{1,0:T(4,128)} %refs_5_.1, s32[2,64]{1,0:T(2,128)} %refs_6_.1, ...), custom_call_target="tpu_custom_call" | custom-call | tf_op jit(solution)/shard_map/pallas_call | solution.py:385
  23.2 1.8 %copy.13 = f32[32,3,1024]{2,0,1:T(8,128)} copy(f32[32,3,1024]{2,0,1:T(8,128)} %bitcast.17) | data formatting | bytes 786432
  25.0 1.3 %copy.14 = f32[32,32]{1,0:T(8,128)} copy(f32[32,32]{1,0:T(8,128)} %get-tuple-element.9) | data formatting | bytes 8192
